TPU v7x, 1024 devices: a whole 8x8x8 slice. The times are simulated.
1024 devices in a mesh: expert: 64 (over x, y), dp: 16 (over z, core).
Axes of the slice: x: 8, y: 8, z: 8, core: 2. Of those that a mesh axis runs over, the one named last changes fastest.
Arguments:
- tokens: bfloat16 [2048, 7168], P('expert', 'dp'), may hold values from -6 to 6
- cotangent: bfloat16 [2048, 7168], P('expert', 'dp'), may hold values from -6 to 6
- expert_ids: int32 [2048, 8], P('expert'), may hold values from 0 to 63, all different within a row; in each aligned block of 32 rows (0 to 31, 32 to 63, ...) at most 8 rows name the same one
- route_weight: float32 [2048, 8], P('expert'), may hold values from 0.1 to 1
- gate_weight: bfloat16 [64, 7168, 1024], P('expert', 'dp'), may hold values from -0.0625 to 0.0625
- up_weight: bfloat16 [64, 7168, 1024], P('expert', 'dp'), may hold values from -0.0625 to 0.0625
- down_weight: bfloat16 [64, 7168, 1024], P('expert', 'dp'), may hold values from -0.1875 to 0.1875
Outputs:
- mixed: bfloat16 [2048, 7168], P('expert', 'dp')
- grad_tokens: bfloat16 [2048, 7168], P('expert', 'dp')
Inputs may be any that keep to these rules, and one draw needn't show every extreme that they name: `expert_ids`: each row names 8 different experts. In the rows of one device (aligned blocks of 32 rows) no expert is named more than 8 times, and in every draw some block names some expert exactly 8 times.
All inputs are finite; a program needn't handle non-finite values.
Results may differ from a plain program's by a relative error of at most 0.028.
Values may be sent and summed in bfloat16 or wider, within the bound.
A program may use at most 32 MiB of HBM per device.

v0:
```python
import jax
import jax.numpy as jnp
from jax import lax
from jax.sharding import PartitionSpec as P


def activate(gate_sum, up_sum):
    return (gate_sum * jax.nn.sigmoid(gate_sum) * up_sum).astype(jnp.bfloat16)


def backprop(hidden_grad, gate_sum, up_sum):
    sig_gate = jax.nn.sigmoid(gate_sum)
    up_grad = (hidden_grad * gate_sum * sig_gate).astype(jnp.bfloat16)
    gate_grad = (hidden_grad * up_sum * sig_gate * (1.0 + gate_sum * (1.0 - sig_gate))).astype(
        jnp.bfloat16
    )
    return (gate_grad, up_grad)


def local(tokens, cotangent, expert_ids, route_weight, gate_weight, up_weight, down_weight):
    experts = lax.axis_size("expert")
    tok_count, share_width = tokens.shape
    top_count = expert_ids.shape[1]
    capacity = max(2, min(tok_count, 2 * tok_count * top_count // experts))
    flat_ids = expert_ids.reshape(-1)
    onehot = (flat_ids[:, None] == jnp.arange(experts, dtype=jnp.int32)[None, :]).astype(jnp.int32)
    before = jnp.cumsum(onehot, axis=0) - onehot
    target = flat_ids * capacity + jnp.sum(before * onehot, axis=1)
    flat_weight = route_weight.reshape(-1)
    token_rows = jnp.repeat(tokens, top_count, axis=0)
    grad_rows = (
        flat_weight[:, None] * jnp.repeat(cotangent, top_count, axis=0).astype(jnp.float32)
    ).astype(jnp.bfloat16)
    empty = jnp.zeros((experts * capacity, share_width), jnp.bfloat16)
    send_tokens = empty.at[target].set(token_rows)
    send_grads = empty.at[target].set(grad_rows)
    routed_tokens, routed_grads = (
        lax.all_to_all(send_tokens, "expert", split_axis=0, concat_axis=0, tiled=True),
        lax.all_to_all(send_grads, "expert", split_axis=0, concat_axis=0, tiled=True),
    )
    gate_w = gate_weight[0]
    up_w = up_weight[0]
    down_w = down_weight[0]
    gate_part = jnp.dot(routed_tokens, gate_w, preferred_element_type=jnp.float32)
    up_part = jnp.dot(routed_tokens, up_w, preferred_element_type=jnp.float32)
    hidden_part = jnp.dot(routed_grads, down_w, preferred_element_type=jnp.float32)
    gate_sum, up_sum = (
        lax.psum_scatter(
            gate_part.astype(jnp.bfloat16), "dp", scatter_dimension=1, tiled=True
        ).astype(jnp.float32),
        lax.psum_scatter(
            up_part.astype(jnp.bfloat16), "dp", scatter_dimension=1, tiled=True
        ).astype(jnp.float32),
    )
    hidden = lax.all_gather(activate(gate_sum, up_sum), "dp", axis=1, tiled=True)
    hidden_grad = lax.psum_scatter(
        hidden_part.astype(jnp.bfloat16), "dp", scatter_dimension=1, tiled=True
    ).astype(jnp.float32)
    gate_share, up_share = backprop(hidden_grad, gate_sum, up_sum)
    gate_grad, up_grad = (
        lax.all_gather(gate_share, "dp", axis=1, tiled=True),
        lax.all_gather(up_share, "dp", axis=1, tiled=True),
    )
    contract = (((1,), (1,)), ((), ()))
    expert_out = lax.dot_general(
        hidden, down_w, contract, preferred_element_type=jnp.float32
    ).astype(jnp.bfloat16)
    slot_grad = (
        lax.dot_general(gate_grad, gate_w, contract, preferred_element_type=jnp.float32)
        + lax.dot_general(up_grad, up_w, contract, preferred_element_type=jnp.float32)
    ).astype(jnp.bfloat16)
    back_out, back_grad = (
        lax.all_to_all(expert_out, "expert", split_axis=0, concat_axis=0, tiled=True),
        lax.all_to_all(slot_grad, "expert", split_axis=0, concat_axis=0, tiled=True),
    )
    picked = back_out[target].astype(jnp.float32) * flat_weight[:, None]
    mixed = jnp.sum(picked.reshape(tok_count, top_count, share_width), axis=1).astype(jnp.bfloat16)
    grad_tokens = jnp.sum(
        back_grad[target].astype(jnp.float32).reshape(tok_count, top_count, share_width), axis=1
    ).astype(jnp.bfloat16)
    return (mixed, grad_tokens)


def solution(mesh):
    return jax.shard_map(
        local,
        mesh=mesh,
        in_specs=(
            P("expert", "dp"),
            P("expert", "dp"),
            P("expert", None),
            P("expert", None),
            P("expert", "dp", None),
            P("expert", "dp", None),
            P("expert", "dp", None),
        ),
        out_specs=(P("expert", "dp"), P("expert", "dp")),
        check_vma=False,
    )
```

profile of v0, /device:TPU:4, one launch (start us, length us, event | category | flops | bytes accessed | tf_op | source)
XLA Modules:
  0.0 428.7 jit_solution(3678642421459476972)
XLA Ops:
  7.2 0.8 broadcast_multiply_fusion
  8.0 0.8 copy.13
  9.2 0.6 reduce-window.6
  10.1 1.9 scatter_custom_fusion
  12.0 32.8 %all_to_all.48 = bf16[64,8,448]{2,1,0:T(8,128)(2,1)S(1)} all-to-all(bf16[64,8,448]{2,1,0:T(8,128)(2,1)S(1)} %bitcast.68), channel_id=1, replica_groups=mesh['expert'=64,'dp'=16] {'expert'}, dimensions={0} | all-to-all | bytes 917504 | tf_op jit(solution)/shard_map/all_to_all | solution.py:38
  44.9 1.7 convolution_convert_fusion.2
  46.7 0.7 copy-done.1
  47.6 1.7 scatter_custom_fusion.1
  49.3 20.5 %all_to_all.49 = bf16[64,8,448]{2,1,0:T(8,128)(2,1)S(1)} all-to-all(bf16[64,8,448]{2,1,0:T(8,128)(2,1)S(1)} %bitcast.69), channel_id=1, replica_groups=mesh['expert'=64,'dp'=16] {'expert'}, dimensions={0} | all-to-all | bytes 917504 | tf_op jit(solution)/shard_map/all_to_all | solution.py:39
  69.8 1.8 convolution_convert_fusion
  71.7 2.9 convolution_convert_fusion.1
  74.7 39.9 %reduce-scatter.4.cloned.1.call-done = bf16[512,64]{0,1:T(8,128)(2,1)} async-done(((bf16[512,1024]{0,1:T(8,128)(2,1)}), bf16[512,64]{0,1:T(8,128)(2,1)}) %reduce-scatter.4.cloned.1.call-update) | async-done | bytes 65552 | tf_op jit(solution)/shard_map/reduce_scatter | solution.py:48
  114.7 65.2 %reduce-scatter.8.cloned.1.call-done = bf16[512,64]{0,1:T(8,128)(2,1)} async-done(((bf16[512,1024]{0,1:T(8,128)(2,1)}), bf16[512,64]{0,1:T(8,128)(2,1)}) %reduce-scatter.8.cloned.1.call-update) | async-done | bytes 65552 | tf_op jit(solution)/shard_map/reduce_scatter | solution.py:56
  179.9 65.2 %reduce-scatter.6.cloned.1.call-done = bf16[512,64]{0,1:T(8,128)(2,1)} async-done(((bf16[512,1024]{0,1:T(8,128)(2,1)}), bf16[512,64]{0,1:T(8,128)(2,1)}) %reduce-scatter.6.cloned.1.call-update) | async-done | bytes 65552 | tf_op jit(solution)/shard_map/reduce_scatter | solution.py:51
  245.1 1.7 fusion.30
  246.8 0.5 all-gather.6.cloned.1.call-update
  247.4 0.5 all-gather.8.cloned.1.call-update
  247.9 43.1 %all-gather.4.cloned.1.call-done = bf16[512,1024]{0,1:T(8,128)(2,1)} async-done(((bf16[512,64]{0,1:T(8,128)(2,1)}), bf16[512,1024]{0,1:T(8,128)(2,1)}) %all-gather.4.cloned.1.call-update) | async-done | bytes 1048592 | tf_op jit(solution)/shard_map/all_gather | solution.py:55
  291.1 1.9 convolution_convert_fusion.3
  292.9 1.0 copy.16
  293.9 12.8 %all-to-all-start.1 = ((bf16[64,8,448]{2,1,0:T(8,128)(2,1)}), bf16[64,8,448]{2,1,0:T(8,128)(2,1)S(1)}, u32[]{:S(2)}, u32[]{:S(2)}) async-start(bf16[64,8,448]{2,1,0:T(8,128)(2,1)} %bitcast.9), calls=%async_computation.3 | async-start | bytes 1048576 | tf_op jit(solution)/shard_map/all_to_all | solution.py:73
  306.7 30.9 %all-gather.6.cloned.1.call-done = bf16[512,1024]{0,1:T(8,128)(2,1)} async-done(((bf16[512,64]{0,1:T(8,128)(2,1)}), bf16[512,1024]{0,1:T(8,128)(2,1)}) %all-gather.6.cloned.1.call-update) | async-done | bytes 1048592 | tf_op jit(solution)/shard_map/all_gather | solution.py:61
  337.6 2.8 fusion.5
  340.4 43.6 %all-gather.8.cloned.1.call-done = bf16[512,1024]{0,1:T(8,128)(2,1)} async-done(((bf16[512,64]{0,1:T(8,128)(2,1)}), bf16[512,1024]{0,1:T(8,128)(2,1)}) %all-gather.8.cloned.1.call-update) | async-done | bytes 1048592 | tf_op jit(solution)/shard_map/all_gather | solution.py:62
  383.9 2.4 fusion
  386.4 1.0 copy.19
  387.4 12.8 %all-to-all-start.3 = ((bf16[64,8,448]{2,1,0:T(8,128)(2,1)}), bf16[64,8,448]{2,1,0:T(8,128)(2,1)S(1)}, u32[]{:S(2)}, u32[]{:S(2)}) async-start(bf16[64,8,448]{2,1,0:T(8,128)(2,1)} %bitcast.15), calls=%async_computation.6 | async-start | bytes 1048576 | tf_op jit(solution)/shard_map/all_to_all | solution.py:74
  400.1 1.2 gather_fusion
  401.3 0.8 fusion.8
  402.1 17.8 %all-to-all-done.3 = bf16[64,8,448]{2,1,0:T(8,128)(2,1)S(1)} async-done(((bf16[64,8,448]{2,1,0:T(8,128)(2,1)}), bf16[64,8,448]{2,1,0:T(8,128)(2,1)S(1)}, u32[]{:S(2)}, u32[]{:S(2)}) %all-to-all-start.3) | async-done | bytes 458784 | tf_op jit(solution)/shard_map/all_to_all | solution.py:74
  420.0 1.2 gather_fusion.1
  421.1 0.8 bitcast_reduce_fusion
  (32 shorter events, 1.2 us)
Async XLA Ops:
  7.2 62.7 %copy-start = (bf16[1,448,1024]{2,1,0:T(8,128)(2,1)S(1)}, bf16[1,448,1024]{2,1,0:T(8,128)(2,1)}, u32[]{:S(2)}) copy-start(bf16[1,448,1024]{2,1,0:T(8,128)(2,1)} %param.13) | copy-start | bytes 2752516
  7.2 37.7 %copy-start.3 = (bf16[1,448,1024]{2,1,0:T(8,128)(2,1)S(1)}, bf16[1,448,1024]{2,1,0:T(8,128)(2,1)}, u32[]{:S(2)}) copy-start(bf16[1,448,1024]{2,1,0:T(8,128)(2,1)} %param.11) | copy-start | bytes 2752516
  7.2 107.5 %reduce-scatter.4.cloned.1.call-start = ((), (), s32[]{:S(2)}) async-start(), calls=%async_computation.7 | async-start | bytes 1114112 | tf_op jit(solution)/shard_map/reduce_scatter | solution.py:48
  46.6 0.8 copy-start.1
  46.6 0.8 copy-start.2
  46.7 133.2 %reduce-scatter.8.cloned.1.call-start = ((), (), s32[]{:S(2)}) async-start(), calls=%async_computation.10 | async-start | bytes 1114112 | tf_op jit(solution)/shard_map/reduce_scatter | solution.py:56
  71.7 173.4 %reduce-scatter.6.cloned.1.call-start = ((), (), s32[]{:S(2)}) async-start(), calls=%async_computation.8 | async-start | bytes 1114112 | tf_op jit(solution)/shard_map/reduce_scatter | solution.py:51
  74.7 216.4 %all-gather.4.cloned.1.call-start = ((), (), s32[]{:S(2)}) async-start(), calls=%async_computation.9 | async-start | bytes 1114112 | tf_op jit(solution)/shard_map/all_gather | solution.py:55
  246.8 90.8 %all-gather.6.cloned.1.call-start = ((), (), s32[]{:S(2)}) async-start(), calls=%async_computation.11 | async-start | bytes 1114112 | tf_op jit(solution)/shard_map/all_gather | solution.py:61
  247.4 136.6 %all-gather.8.cloned.1.call-start = ((), (), s32[]{:S(2)}) async-start(), calls=%async_computation.12 | async-start | bytes 1114112 | tf_op jit(solution)/shard_map/all_gather | solution.py:62
  293.9 93.4 %all-to-all-start.1 = ((bf16[64,8,448]{2,1,0:T(8,128)(2,1)}), bf16[64,8,448]{2,1,0:T(8,128)(2,1)S(1)}, u32[]{:S(2)}, u32[]{:S(2)}) async-start(bf16[64,8,448]{2,1,0:T(8,128)(2,1)} %bitcast.9), calls=%async_computation.3 | async-start | bytes 1048576 | tf_op jit(solution)/shard_map/all_to_all | solution.py:73
  387.4 32.6 %all-to-all-start.3 = ((bf16[64,8,448]{2,1,0:T(8,128)(2,1)}), bf16[64,8,448]{2,1,0:T(8,128)(2,1)S(1)}, u32[]{:S(2)}, u32[]{:S(2)}) async-start(bf16[64,8,448]{2,1,0:T(8,128)(2,1)} %bitcast.15), calls=%async_computation.6 | async-start | bytes 1048576 | tf_op jit(solution)/shard_map/all_to_all | solution.py:74
Sparse Core Ops, SparseCore 0:
  46.8 67.8 reduce-scatter.3
  118.4 61.3 reduce-scatter.7
  183.3 61.7 reduce-scatter.5
  248.0 43.0 all-gather.3
  294.0 43.5 all-gather.5
  340.5 43.3 all-gather.7
where the time goes:
time: 429 us
  waiting for transfers between devices  307 us (72%)
  blocking collectives  53.4 us (12%)
  starting transfers between devices  25.8 us (6%)
  between operations  14.2 us (3%)
  matrix products  13.6 us (3%)
  local copies, waits for them, and re-layouts  8.34 us (2%)
  other arithmetic  6.62 us (2%)
    reduce_scatter x1, waiting for transfers between devices, local(): lax.psum_scatter(up_part.astype(jnp.bfloat16), 'dp', scatter_dimension=1,...  65.2 us
    reduce_scatter x1, waiting for transfers between devices, local(): lax.psum_scatter(hidden_part.astype(jnp.bfloat16), 'dp', scatter_dimensio...  65.2 us
    all_gather x1, waiting for transfers between devices, local(): lax.all_gather(up_share, 'dp', axis=1, tiled=True)  43.6 us
    all_gather x1, waiting for transfers between devices, local(): lax.all_gather(activate(gate_sum, up_sum), 'dp', axis=1, tiled=True)  43.1 us
    reduce_scatter x1, waiting for transfers between devices, local(): lax.psum_scatter(gate_part.astype(jnp.bfloat16), 'dp', scatter_dimension=...  39.9 us
    all_to_all x1, blocking collectives, local(): lax.all_to_all(send_tokens, 'expert', split_axis=0, concat_axis=0, tiled=...  32.8 us
    all_gather x1, waiting for transfers between devices, local(): lax.all_gather(gate_share, 'dp', axis=1, tiled=True)  30.9 us
    all_to_all x1, blocking collectives, local(): lax.all_to_all(send_grads, 'expert', split_axis=0, concat_axis=0, tiled=T...  20.5 us
  transfers between devices with their start and end apart: 8, of which 7 were waited for; matrix products, arithmetic and copies ran while one was open for 4% of the time, Pallas kernels for 0%

commit v1 on v0

v1 whole, which is shorter than its diff:
```python
import functools
import math

import jax
import jax.numpy as jnp
from jax import lax
from jax.experimental import pallas as pl
from jax.experimental.pallas import tpu as pltpu
from jax.sharding import PartitionSpec as P

MESH = pl.DeviceIdType.MESH
BF = jnp.bfloat16
F32 = jnp.float32


def dot(left, right):
    return jnp.dot(left, right, preferred_element_type=F32)


def dot_t(left, right):
    return lax.dot_general(left, right, (((1,), (1,)), ((), ())), preferred_element_type=F32)


def join(low, high, width):
    part = low.shape[1]
    edge = 2 * width - part
    lanes = lax.broadcasted_iota(jnp.int32, (low.shape[0], part - edge), 1) + edge
    middle = jnp.where(lanes < width, low[:, edge:], high[:, : part - edge])
    if edge == 0:
        return middle
    return jnp.concatenate([low[:, :edge], middle, high[:, part - edge :]], axis=1)


def kernel(
    ne, nz, top, cap, width, rows_ref, meta_ref, gate_ref, up_ref, down_ref, out_ref,
    gath, mgath, wts, keys, kw, pick, pick_hi, pick_lo, sbuf, rbuf, own, sib_out, sib_in,
    acc_a, acc_b, in_a, in_b, hid, obuf, qbuf, cbuf, fbuf,
    w_sem, m_sem, g_sem, r_sem, x_sem, ra_sem, rb_sem, ha_sem, hb_sem, hx_sem, q_sem, f_sem,
    m_snd, g_snd, r_snd, x_snd, ra_snd, rb_snd, ha_snd, hb_snd, hx_snd, q_snd, f_snd,
):
    half = nz // 2
    tok = rows_ref.shape[0]
    pad = wts.shape[1]
    low_cols, high_cols = slice(0, pad), slice(2 * width - pad, 2 * width)
    quarter = hid.shape[3]
    ff = hid.shape[4]
    e = lax.axis_index("expert")
    d = lax.axis_index("dp")
    x, y = e // ne, e % ne
    z, c = d // 2, d % 2
    a = x * (1 - c) + y * c
    b = y * (1 - c) + x * c
    step_a = ne - c * (ne - 1)
    step_b = 1 + c * (ne - 1)
    sign = 1 - 2 * c

    def place(aa, bb):
        return (aa * step_a + bb * step_b, d)

    side = (e, z * 2 + (1 - c))
    next_a = (e, ((z + sign + nz) % nz) * 2 + c)
    next_b = (e, ((z - sign + nz) % nz) * 2 + c)

    def remote(src, dst, send, recv, device):
        pltpu.make_async_remote_copy(
            src_ref=src, dst_ref=dst, send_sem=send, recv_sem=recv, device_id=device, device_id_type=MESH
        ).start()

    def wait(ref, sem):
        pltpu.make_async_copy(ref, ref, sem).wait()

    loads = [
        pltpu.make_async_copy(gate_ref, wts.at[0, pl.ds(0, width)], w_sem.at[0]),
        pltpu.make_async_copy(up_ref, wts.at[1, pl.ds(0, width)], w_sem.at[1]),
        pltpu.make_async_copy(down_ref, wts.at[2, pl.ds(pad - width, width)], w_sem.at[2]),
    ]
    for load in loads:
        load.start()

    barrier = pltpu.get_barrier_semaphore()
    greeted = [place((a + p) % ne, b) for p in range(1, ne)] + [place(a, (b + p) % ne) for p in range(1, ne)]
    greeted += [side, next_a, next_b]
    for device in greeted:
        pl.semaphore_signal(barrier, inc=1, device_id=device, device_id_type=MESH)
    if pad > width:
        blank = jnp.zeros((pad - width, ff), BF)
        wts[0, width:] = blank
        wts[1, width:] = blank
        wts[2, : pad - width] = blank
    pl.semaphore_wait(barrier, len(greeted))

    peers = sorted(range(1, ne), key=lambda p: -min(p, ne - p))
    for p in peers:
        remote(meta_ref, mgath.at[a], m_snd, m_sem, place((a + p) % ne, b))
    pltpu.make_async_copy(meta_ref, mgath.at[a], m_sem).start()
    for p in peers:
        remote(rows_ref, gath.at[a], g_snd, g_sem, place((a + p) % ne, b))
    pltpu.make_async_copy(rows_ref, gath.at[a], g_sem).start()

    wait(mgath, m_sem)
    lanes = mgath.shape[2]
    per = lanes // tok
    lane = lax.broadcasted_iota(jnp.int32, (2 * top, lanes), 1)
    parts = []
    for first in range(0, ne, per):
        total = jnp.zeros((2 * top, lanes), F32)
        for i in range(min(per, ne - first)):
            total = total + jnp.where(lane // tok == i, mgath[first + i], 0.0)
        parts.append(total)
    merged = jnp.concatenate(parts, axis=1) if len(parts) > 1 else parts[0]
    span = merged.shape[1]
    ids, weight = merged[:top], merged[top:]
    named, carried = [], []
    for i in range(ne):
        same = ids == (a * step_a + i * step_b).astype(F32)
        named.append(jnp.sum(same.astype(F32), axis=0, keepdims=True))
        carried.append(jnp.sum(jnp.where(same, weight, 0.0), axis=0, keepdims=True))
    named = jnp.concatenate(named, axis=0)
    row = lax.broadcasted_iota(jnp.int32, (span, span), 0)
    col = lax.broadcasted_iota(jnp.int32, (span, span), 1)
    earlier = ((row // tok == col // tok) & (row < col)).astype(F32).astype(BF)
    slot = dot(named.astype(BF), earlier)
    keys[...] = jnp.where(named > 0.5, slot, -1.0)
    kw[...] = jnp.concatenate(carried, axis=0)

    def choose(i, carry):
        row = lax.broadcasted_iota(jnp.int32, (ne * cap, span), 0)
        col = lax.broadcasted_iota(jnp.int32, (ne * cap, span), 1)
        hit = (keys[pl.ds(i, 1)] == (row % cap).astype(F32)) & (row // cap == col // tok)
        scaled = jnp.where(hit, kw[pl.ds(i, 1)], 0.0)
        high = scaled.astype(BF)
        at = pl.ds(pl.multiple_of(i * (ne * cap), ne * cap), ne * cap)
        pick[at] = hit.astype(F32).astype(BF)
        pick_hi[at] = high
        pick_lo[at] = (scaled - high.astype(F32)).astype(BF)
        return carry

    lax.fori_loop(0, ne, choose, 0)

    wait(gath, g_sem)

    def route(i, carry):
        at = pl.ds(pl.multiple_of(i * (ne * cap), ne * cap), ne * cap)
        source = gath[...].reshape(ne * tok, 2 * width)
        low = dot(pick[at], source[:, low_cols])
        high = dot(pick_hi[at], source[:, high_cols]) + dot(pick_lo[at], source[:, high_cols])
        sbuf[i] = join(low, high, width).reshape(ne, cap, 2 * width).astype(BF)
        return carry

    lax.fori_loop(0, ne, route, 0)

    def chunk(i):
        off = (half - (i + 1) // 2) * (2 * (i % 2) - 1)
        return (z + off + nz) % nz

    def dispatch(i, carry):
        j = chunk(i)

        @pl.when(c == 0)
        def _():
            to = (b - j + ne) % ne

            @pl.when(j == 0)
            def _():
                pltpu.make_async_copy(sbuf.at[b], rbuf.at[0], r_sem.at[0]).start()

            @pl.when(j != 0)
            def _():
                remote(sbuf.at[to], rbuf.at[j], r_snd, r_sem.at[j], place(a, to))

        @pl.when(c == 1)
        def _():
            of = (a + j) % ne
            for p in peers:
                to = (b + p) % ne
                remote(sbuf.at[to, of], rbuf.at[j, b], r_snd, r_sem.at[j], place(a, to))
            pltpu.make_async_copy(sbuf.at[b, of], rbuf.at[j, b], r_sem.at[j]).start()

        return carry

    lax.fori_loop(0, nz, dispatch, 0)
    for load in loads:
        load.wait()

    def forward(i, carry):
        j = chunk(i)
        wait(rbuf.at[j], r_sem.at[j])
        rows = rbuf[j].astype(F32).reshape(ne * cap, 2 * width)
        rows_low = rows[:, low_cols].astype(BF)
        rows_high = rows[:, high_cols].astype(BF)
        for p in range(3):
            part = dot(rows_low if p < 2 else rows_high, wts[p])
            first, second = part[:quarter], part[quarter:]
            swap = jnp.broadcast_to(c, first.shape) == 1
            own[p, j] = jnp.where(swap, second, first)
            sib_out[p, j] = jnp.where(swap, first, second).astype(BF)
            remote(sib_out.at[p, j], sib_in.at[p, j], x_snd, x_sem.at[p, j], side)
        return carry

    def both(p, j):
        wait(sib_in.at[p, j], x_sem.at[p, j])
        return own[p, j] + sib_in[p, j].astype(F32)

    lax.fori_loop(0, 3, forward, 0)
    done = 3
    for m in range(half):
        for p in range(3):
            value = both(p, (z + sign * (half - m) + nz) % nz)
            if m > 0:
                wait(in_a.at[m - 1, p], ra_sem.at[m - 1, p])
                value = value + in_a[m - 1, p].astype(F32)
            acc_a[m, p] = value.astype(BF)
            remote(acc_a.at[m, p], in_a.at[m, p], ra_snd, ra_sem.at[m, p], next_a)
            if m < half - 1:
                value = both(p, (z - sign * (half - 1 - m) + nz) % nz)
                if m > 0:
                    wait(in_b.at[m - 1, p], rb_sem.at[m - 1, p])
                    value = value + in_b[m - 1, p].astype(F32)
                acc_b[m, p] = value.astype(BF)
                remote(acc_b.at[m, p], in_b.at[m, p], rb_snd, rb_sem.at[m, p], next_b)
        more = min(nz, done + 2)
        if more > done:
            lax.fori_loop(done, more, forward, 0)
        done = more

    for p in range(3):
        wait(sib_in.at[p, z], x_sem.at[p, z])
        wait(in_b.at[half - 2, p], rb_sem.at[half - 2, p])
        wait(in_a.at[half - 1, p], ra_sem.at[half - 1, p])

    def activate(q, carry):
        at = pl.ds(pl.multiple_of(q * 128, 128), 128)

        def total(p):
            value = own[p, z, :, at] + sib_in[p, z, :, at].astype(F32)
            return value + in_a[half - 1, p, :, at].astype(F32) + in_b[half - 2, p, :, at].astype(F32)

        gate, up, grad = total(0), total(1), total(2)
        sig = jax.nn.sigmoid(gate)
        hid[0, z, c, :, at] = (gate * sig * up).astype(BF)
        hid[1, z, c, :, at] = (grad * up * sig * (1.0 + gate * (1.0 - sig))).astype(BF)
        hid[2, z, c, :, at] = (grad * gate * sig).astype(BF)
        return carry

    lax.fori_loop(0, ff // 128, activate, 0)

    def share(p, j):
        remote(hid.at[p, j, c], hid.at[p, j, c], hx_snd, hx_sem.at[p, j], side)

    def backward(j):
        for p in range(3):
            wait(hid.at[p, j, 1 - c], hx_sem.at[p, j])
        acts = [hid[p, j].reshape(2 * quarter, ff) for p in range(3)]
        low = dot_t(acts[1], wts[0]) + dot_t(acts[2], wts[1])
        high = dot_t(acts[0], wts[2])
        obuf[j] = join(low, high, width).reshape(ne, cap, 2 * width).astype(BF)

        @pl.when(c == 0)
        def _():
            to = (b + j) % ne

            @pl.when(j == 0)
            def _():
                pltpu.make_async_copy(obuf.at[0], qbuf.at[b], q_sem).start()

            @pl.when(j != 0)
            def _():
                remote(obuf.at[j], qbuf.at[b], q_snd, q_sem, place(a, to))

        @pl.when(c == 1)
        def _():
            of = (a + j) % ne
            for p in peers:
                to = (b + p) % ne
                remote(obuf.at[j, to], qbuf.at[b, of], q_snd, q_sem, place(a, to))
            pltpu.make_async_copy(obuf.at[j, b], qbuf.at[b, of], q_sem).start()

    for p in range(3):
        remote(hid.at[p, z, c], hid.at[p, z, c], ha_snd, ha_sem.at[0, p], next_a)
        remote(hid.at[p, z, c], hid.at[p, z, c], hb_snd, hb_sem.at[0, p], next_b)
        share(p, z)
    for k in range(1, half + 1):
        for p in range(3):
            j = (z - sign * k + nz) % nz
            wait(hid.at[p, j, c], ha_sem.at[k - 1, p])
            if k < half:
                remote(hid.at[p, j, c], hid.at[p, j, c], ha_snd, ha_sem.at[k, p], next_a)
            share(p, j)
            if k < half:
                j = (z + sign * k + nz) % nz
                wait(hid.at[p, j, c], hb_sem.at[k - 1, p])
                if k < half - 1:
                    remote(hid.at[p, j, c], hid.at[p, j, c], hb_snd, hb_sem.at[k, p], next_b)
                share(p, j)
        if k == 1:
            backward(z)
        else:

            def pair(i, carry, k=k):
                backward((z + (k - 1) * (1 - 2 * i) + nz) % nz)
                return carry

            lax.fori_loop(0, 2, pair, 0)
    backward((z + half) % nz)

    wait(qbuf, q_sem)
    back = qbuf[...].astype(F32).reshape(ne * ne * cap, 2 * width)
    across = (((0,), (0,)), ((), ()))
    back_low, back_high = back[:, low_cols].astype(BF), back[:, high_cols].astype(BF)
    low = lax.dot_general(pick[...], back_low, across, preferred_element_type=F32)
    high = lax.dot_general(pick_hi[...], back_high, across, preferred_element_type=F32)
    high = high + lax.dot_general(pick_lo[...], back_high, across, preferred_element_type=F32)
    cbuf[...] = join(low, high, width).astype(BF).reshape(ne, tok, 2 * width)
    for p in peers:
        to = (a + p) % ne
        remote(cbuf.at[to], fbuf.at[a], f_snd, f_sem, place(to, b))
    pltpu.make_async_copy(cbuf.at[a], fbuf.at[a], f_sem).start()
    wait(fbuf, f_sem)
    total = fbuf[0].astype(F32)
    for i in range(1, ne):
        total = total + fbuf[i].astype(F32)
    out_ref[...] = total.astype(BF)

    wait(mgath.at[pl.ds(0, ne - 1)], m_snd)
    wait(gath.at[pl.ds(0, ne - 1)], g_snd)
    wait(sbuf.at[pl.ds(0, ne - 1)], r_snd)
    wait(obuf.at[pl.ds(0, nz - 1)], q_snd)
    wait(cbuf.at[pl.ds(0, ne - 1)], f_snd)
    wait(sib_out, x_snd)
    wait(acc_a, ra_snd)
    wait(acc_b, rb_snd)
    wait(hid.at[:, pl.ds(0, half), 0], ha_snd)
    wait(hid.at[:, pl.ds(0, half - 1), 0], hb_snd)
    wait(hid.at[:, :, 0], hx_snd)


def local(ne, nz, tokens, cotangent, expert_ids, route_weight, gate_weight, up_weight, down_weight):
    tok, width = tokens.shape
    top = expert_ids.shape[1]
    ff = gate_weight.shape[2]
    cap = max(2, min(tok, 2 * tok * top // (ne * ne)))
    pad = -(-width // 128) * 128
    quarter = ne * cap // 2
    rows = jnp.concatenate([tokens, cotangent], axis=1)
    meta = jnp.concatenate([expert_ids.astype(F32), route_weight], axis=1).T
    meta = jnp.tile(meta, (1, 128 // tok))
    span = -(-ne // (128 // tok)) * 128
    half = nz // 2
    dma = pltpu.SemaphoreType.DMA
    scratch = [
        pltpu.VMEM((ne, tok, 2 * width), BF),
        pltpu.VMEM((ne, 2 * top, 128), F32),
        pltpu.VMEM((3, pad, ff), BF),
        pltpu.VMEM((ne, span), F32),
        pltpu.VMEM((ne, span), F32),
        pltpu.VMEM((ne * ne * cap, span), BF),
        pltpu.VMEM((ne * ne * cap, span), BF),
        pltpu.VMEM((ne * ne * cap, span), BF),
        pltpu.VMEM((ne, ne, cap, 2 * width), BF),
        pltpu.VMEM((nz, ne, cap, 2 * width), BF),
        pltpu.VMEM((3, nz, quarter, ff), F32),
        pltpu.VMEM((3, nz, quarter, ff), BF),
        pltpu.VMEM((3, nz, quarter, ff), BF),
        pltpu.VMEM((half, 3, quarter, ff), BF),
        pltpu.VMEM((half - 1, 3, quarter, ff), BF),
        pltpu.VMEM((half, 3, quarter, ff), BF),
        pltpu.VMEM((half - 1, 3, quarter, ff), BF),
        pltpu.VMEM((3, nz, 2, quarter, ff), BF),
        pltpu.VMEM((nz, ne, cap, 2 * width), BF),
        pltpu.VMEM((ne, ne, cap, 2 * width), BF),
        pltpu.VMEM((ne, tok, 2 * width), BF),
        pltpu.VMEM((ne, tok, 2 * width), BF),
        dma((3,)),
        dma,
        dma,
        dma((nz,)),
        dma((3, nz)),
        dma((half, 3)),
        dma((half - 1, 3)),
        dma((half, 3)),
        dma((half - 1, 3)),
        dma((3, nz)),
        dma,
        dma,
    ] + [dma] * 11
    vmem, anywhere = pl.BlockSpec(memory_space=pltpu.VMEM), pl.BlockSpec(memory_space=pl.ANY)
    out = pl.pallas_call(
        functools.partial(kernel, ne, nz, top, cap, width),
        out_shape=jax.ShapeDtypeStruct((tok, 2 * width), BF),
        in_specs=[vmem, vmem, anywhere, anywhere, anywhere],
        out_specs=vmem,
        scratch_shapes=scratch,
        compiler_params=pltpu.CompilerParams(
            collective_id=0, has_side_effects=True, vmem_limit_bytes=50 * 2**20
        ),
    )(rows, meta, gate_weight[0], up_weight[0], down_weight[0])
    return out[:, width:], out[:, :width]


def solution(mesh):
    ne = math.isqrt(mesh.shape["expert"])
    nz = mesh.shape["dp"] // 2
    return jax.shard_map(
        functools.partial(local, ne, nz),
        mesh=mesh,
        in_specs=(
            P("expert", "dp"),
            P("expert", "dp"),
            P("expert", None),
            P("expert", None),
            P("expert", "dp", None),
            P("expert", "dp", None),
            P("expert", "dp", None),
        ),
        out_specs=(P("expert", "dp"), P("expert", "dp")),
        check_vma=False,
    )
```

time: 429 us -> 117 us (0.27)
  the two profiles are of different devices: /device:TPU:4 before, /device:TPU:16 now
where the time goes in v1:
time: 117 us
  Pallas kernels  110 us (94%)
  local copies, waits for them, and re-layouts  6.36 us (5%)
    pallas_call x1, Pallas kernels, local(): pl.pallas_call(functools.partial(kernel, ne, nz, top, cap, width), out_sh...  110 us
    unnamed x14, local copies, waits for them, and re-layouts  5.57 us

profile of v1, /device:TPU:16, one launch (start us, length us, event | category | flops | bytes accessed | tf_op | source)
XLA Modules:
  0.0 116.6 jit_solution(2596808154599782094)
XLA Ops:
  0.6 0.0 copy-start.5
  0.6 0.7 copy-done.5
  1.3 0.0 copy-start.6
  1.3 0.7 copy-done.6
  2.0 0.0 copy-start.3
  2.0 0.0 copy-start.4
  2.0 0.1 tile.10.meta_ref
  2.1 0.7 copy-done.3
  2.8 0.0 copy-done.4
  2.8 0.1 pad_maximum_fusion.rows_ref
  2.9 0.0 copy-start
  2.9 1.2 %copy-done = bf16[1,448,1024]{2,1,0:T(8,128)(2,1)S(1)} copy-done((bf16[1,448,1024]{2,1,0:T(8,128)(2,1)S(1)}, bf16[1,448,1024]{2,1,0:T(8,128)(2,1)}, u32[]{:S(2)}) %copy-start) | copy-done | bytes 917528
  4.0 0.0 copy-start.1
  4.0 1.2 %copy-done.1 = bf16[1,448,1024]{2,1,0:T(8,128)(2,1)S(1)} copy-done((bf16[1,448,1024]{2,1,0:T(8,128)(2,1)S(1)}, bf16[1,448,1024]{2,1,0:T(8,128)(2,1)}, u32[]{:S(2)}) %copy-start.1) | copy-done | bytes 917528
  5.2 0.0 copy-start.2
  5.2 1.2 %copy-done.2 = bf16[1,448,1024]{2,1,0:T(8,128)(2,1)S(1)} copy-done((bf16[1,448,1024]{2,1,0:T(8,128)(2,1)S(1)}, bf16[1,448,1024]{2,1,0:T(8,128)(2,1)}, u32[]{:S(2)}) %copy-start.2) | copy-done | bytes 917528
  6.4 109.5 %shard_map.86 = bf16[32,896]{1,0:T(8,128)(2,1)S(1)} custom-call(bf16[32,896]{1,0:T(8,128)(2,1)S(1)} %pad_maximum_fusion.rows_ref, f32[16,128]{1,0:T(8,128)S(1)} %tile.10.meta_ref, bf16[448,1024]{1,0:T(8,128)(2,1)S(1)} %bitcast.5, bf16[448,1024]{1,0:T(8,128)(2,1)S(1)} %bitcast.6, bf16[448,1024]{1,0:T(8,128)(2,1)S(1)} %bitcast.7), custom_call_target="tpu_custom_call" | custom-call | tf_op jit(solution)/shard_map/pallas_call | solution.py:387
  115.9 0.7 fusion
  (3 shorter events, 0.0 us)
Async XLA Ops:
  0.6 0.7 copy-start.5
  1.3 0.7 copy-start.6
  2.0 0.8 copy-start.3
  2.0 0.8 copy-start.4
  2.9 1.2 %copy-start = (bf16[1,448,1024]{2,1,0:T(8,128)(2,1)S(1)}, bf16[1,448,1024]{2,1,0:T(8,128)(2,1)}, u32[]{:S(2)}) copy-start(bf16[1,448,1024]{2,1,0:T(8,128)(2,1)} %param.11) | copy-start | bytes 2752516
  4.0 1.2 %copy-start.1 = (bf16[1,448,1024]{2,1,0:T(8,128)(2,1)S(1)}, bf16[1,448,1024]{2,1,0:T(8,128)(2,1)}, u32[]{:S(2)}) copy-start(bf16[1,448,1024]{2,1,0:T(8,128)(2,1)} %param.12) | copy-start | bytes 2752516
  5.2 1.2 %copy-start.2 = (bf16[1,448,1024]{2,1,0:T(8,128)(2,1)S(1)}, bf16[1,448,1024]{2,1,0:T(8,128)(2,1)}, u32[]{:S(2)}) copy-start(bf16[1,448,1024]{2,1,0:T(8,128)(2,1)} %param.13) | copy-start | bytes 2752516
